TPU v7x, 256 devices: a whole 4x4x8 slice. The times are simulated.
256 devices in a mesh: ctx: 32 (over z_lo, y, x), exp: 8 (over z_hi, core).
Axes of the slice: x: 4, y: 4, z: 8 (z_hi: 4, z_lo: 2; z = z_hi * 2 + z_lo), core: 2. Of those that a mesh axis runs over, the one named last changes fastest.
Arguments:
- tokens: bfloat16 [4096, 2880], P('ctx'), may hold values from -6 to 6
- cotangent: bfloat16 [4096, 2880], P('ctx'), may hold values from -6 to 6
- expert_ids: int32 [4096, 4], P('ctx'), may hold values from 0 to 31, all different within a row; in each aligned block of 128 rows (0 to 127, 128 to 255, ...) at most 20 rows name the same one
- combine_weights: float32 [4096, 4], P('ctx'), may hold values from 0.05 to 1
- w_query: bfloat16 [2880, 2048], P('ctx', 'exp'), may hold values from -0.109375 to 0.109375
- key_value_weight: bfloat16 [2880, 1024], P('ctx', 'exp'), may hold values from -0.109375 to 0.109375
- w_output: bfloat16 [2048, 2880], P('exp', 'ctx'), may hold values from -0.125 to 0.125
- w_gate: bfloat16 [32, 2880, 2048], P('ctx', None, 'exp'), may hold values from -0.109375 to 0.109375
- w_up: bfloat16 [32, 2880, 2048], P('ctx', None, 'exp'), may hold values from -0.109375 to 0.109375
- w_down: bfloat16 [32, 2048, 2880], P('ctx', 'exp'), may hold values from -0.125 to 0.125
Outputs:
- block_out: bfloat16 [4096, 2880], P('ctx')
- grad_tokens: bfloat16 [4096, 2880], P('ctx')
- grad_query: bfloat16 [2880, 2048], P('ctx', 'exp')
- grad_keyval: bfloat16 [2880, 1024], P('ctx', 'exp')
- grad_output: bfloat16 [2048, 2880], P('exp', 'ctx')
- grad_gate: bfloat16 [32, 2880, 2048], P('ctx', None, 'exp')
- grad_up: bfloat16 [32, 2880, 2048], P('ctx', None, 'exp')
- grad_down: bfloat16 [32, 2048, 2880], P('ctx', 'exp')
Inputs may be any that keep to these rules, and one draw needn't show every extreme that they name: `expert_ids`: each row names 4 different experts. Within the 128 rows of one context block no expert is named more than 20 times, and in some block one expert is named exactly 20 times.
All inputs are finite; a program needn't handle non-finite values.
Results may differ from a plain program's by a relative error of at most 0.029.
Values may be sent and summed in bfloat16 or wider, within the bound.
A program may use at most 128 MiB of HBM per device.

v0:
```python
import jax
import jax.numpy as jnp
from jax import lax
from jax.sharding import PartitionSpec as P

QUERY_HEADS = 32
KEY_VALUE_HEADS = 8
HEAD_SIZE = 64
WINDOW = 128
EPSILON = 1e-05
GLU_ALPHA = 1.702


def shifted(shard, axis, by):
    size = lax.axis_size(axis)
    pairs = [(i, i + by) for i in range(size) if 0 <= i + by < size]
    return lax.ppermute(shard, axis, pairs)


def rms_norm(values):
    inv_rms = lax.rsqrt(jnp.mean(values * values, axis=-1, keepdims=True) + EPSILON)
    return (values * inv_rms, inv_rms)


def rms_back(values, inv_rms, grad_in):
    inner_mean = jnp.mean(grad_in * values, axis=-1, keepdims=True)
    return inv_rms * grad_in - values * (inv_rms * inv_rms * inv_rms) * inner_mean


def rounded(values):
    return lax.optimization_barrier(values.astype(jnp.bfloat16)).astype(jnp.float32)


def band_valid(row_count, band_width, block_idx):
    query_pos = block_idx * row_count + jnp.arange(row_count)[:, None]
    key_pos = block_idx * row_count - band_width + jnp.arange(band_width + row_count)[None, :]
    return (key_pos <= query_pos) & (key_pos > query_pos - band_width) & (key_pos >= 0)


def attend(query_matrix, key_value, valid_mask):
    key_rows = key_value[:, :, 0]
    value_rows = key_value[:, :, 1]
    scores = (
        jnp.einsum("tgjd,sgd->gjts", query_matrix, key_rows, preferred_element_type=jnp.float32)
        * 0.125
    )
    weights = jnp.where(valid_mask, jnp.exp(scores), 0.0)
    probability_single = weights / jnp.sum(weights, axis=-1, keepdims=True)
    probability_half = probability_single.astype(jnp.bfloat16)
    attended = jnp.einsum(
        "gjts,sgd->tgjd", probability_half, value_rows, preferred_element_type=jnp.float32
    )
    return (attended.astype(jnp.bfloat16), probability_single, probability_half)


def attention_backward(query_matrix, key_value, probability_single, probability_half, grad_out):
    key_rows = key_value[:, :, 0]
    value_rows = key_value[:, :, 1]
    grad_prob = jnp.einsum(
        "tgjd,sgd->gjts", grad_out, value_rows, preferred_element_type=jnp.float32
    )
    grad_value = jnp.einsum(
        "gjts,tgjd->sgd", probability_half, grad_out, preferred_element_type=jnp.float32
    )
    grad_score = (
        probability_single
        * (grad_prob - jnp.sum(grad_prob * probability_single, axis=-1, keepdims=True))
        * 0.125
    ).astype(jnp.bfloat16)
    query_gradients = jnp.einsum(
        "gjts,sgd->tgjd", grad_score, key_rows, preferred_element_type=jnp.float32
    )
    grad_key = jnp.einsum(
        "gjts,tgjd->sgd", grad_score, query_matrix, preferred_element_type=jnp.float32
    )
    return (query_gradients, jnp.stack([grad_key, grad_value], axis=2))


def place_routes(flat_ids, expert_count, capacity):
    one_hot = (flat_ids[:, None] == jnp.arange(expert_count)[None, :]).astype(jnp.int32)
    earlier = jnp.cumsum(one_hot, axis=0) - one_hot
    return flat_ids * capacity + jnp.sum(earlier * one_hot, axis=1)


def pick_rows(returned, route_table):
    feature_count = returned.shape[-1]
    flat_slots = returned.reshape(-1, feature_count)
    return jnp.einsum("tks,sd->tkd", route_table, flat_slots, preferred_element_type=jnp.float32)


def sum_heads(values):
    return lax.psum(values.astype(jnp.bfloat16), "exp").astype(jnp.float32)


def over_experts(buffer):
    return lax.all_to_all(buffer, "ctx", split_axis=0, concat_axis=0, tiled=True)


def back_from_experts(buffer):
    return lax.all_to_all(buffer, "ctx", split_axis=0, concat_axis=0, tiled=True)


def body(
    tokens,
    cotangent,
    expert_ids,
    combine_weights,
    w_query,
    key_value_weight,
    w_output,
    w_gate,
    w_up,
    w_down,
):
    row_count, model_width = tokens.shape
    top_count = expert_ids.shape[1]
    ctx_count = lax.axis_size("ctx")
    ctx_block = lax.axis_index("ctx")
    capacity = row_count * top_count * 5 // (4 * ctx_count)
    kv_heads = key_value_weight.shape[1] // (2 * HEAD_SIZE)
    query_head_group = QUERY_HEADS // KEY_VALUE_HEADS
    tokens_f32 = tokens.astype(jnp.float32)
    normed_f32, token_scale = rms_norm(tokens_f32)
    normed = normed_f32.astype(jnp.bfloat16)
    full_query, full_keyval, full_output = (
        lax.all_gather(w_query, "ctx", axis=0, tiled=True),
        lax.all_gather(key_value_weight, "ctx", axis=0, tiled=True),
        lax.all_gather(w_output, "ctx", axis=1, tiled=True),
    )
    query_matrix = jnp.dot(normed, full_query, preferred_element_type=jnp.float32).astype(
        jnp.bfloat16
    )
    key_value = jnp.dot(normed, full_keyval, preferred_element_type=jnp.float32).astype(
        jnp.bfloat16
    )
    prev_rim = shifted(key_value, "ctx", 1)
    query_heads = query_matrix.reshape(row_count, kv_heads, query_head_group, HEAD_SIZE)
    banded_key_span = jnp.concatenate([prev_rim, key_value], axis=0).reshape(
        WINDOW + row_count, kv_heads, 2, HEAD_SIZE
    )
    valid_mask = band_valid(row_count, WINDOW, ctx_block)
    attended, probability_single, probability_half = attend(
        query_heads, banded_key_span, valid_mask
    )
    attended_flat = attended.reshape(row_count, -1)
    head_part = jnp.dot(attended_flat, full_output, preferred_element_type=jnp.float32)
    residual = (tokens_f32 + sum_heads(head_part)).astype(jnp.bfloat16)
    moe_f32, resid_scale = rms_norm(residual.astype(jnp.float32))
    moe_input = moe_f32.astype(jnp.bfloat16)
    residual_f32 = residual.astype(jnp.float32)
    slot_count = ctx_count * capacity
    target = place_routes(expert_ids.reshape(-1), ctx_count, capacity)
    route_table = (
        (target[:, None] == jnp.arange(slot_count)[None, :])
        .astype(jnp.bfloat16)
        .reshape(row_count, top_count, slot_count)
    )
    slot_token = jnp.sum(route_table, axis=1)
    outgoing = jnp.dot(slot_token.T, moe_input, preferred_element_type=jnp.float32).astype(
        jnp.bfloat16
    )
    incoming = over_experts(outgoing.reshape(ctx_count, capacity, model_width))
    expert_rows = incoming.reshape(-1, model_width)
    gate_pre = jnp.dot(expert_rows, w_gate[0], preferred_element_type=jnp.float32)
    up_pre = jnp.dot(expert_rows, w_up[0], preferred_element_type=jnp.float32)
    gate_sig = jax.nn.sigmoid(GLU_ALPHA * gate_pre)
    gate_glu = gate_pre * gate_sig
    activated = (gate_glu * (up_pre + 1.0)).astype(jnp.bfloat16)
    down_part = (
        jnp.dot(activated, w_down[0], preferred_element_type=jnp.float32)
        .astype(jnp.bfloat16)
        .reshape(ctx_count, capacity, model_width)
    )
    route_scale = combine_weights[:, :, None]
    returned = back_from_experts(down_part)
    moe_total = sum_heads(jnp.sum(pick_rows(returned, route_table) * route_scale, axis=1))
    block_out = (residual_f32 + moe_total).astype(jnp.bfloat16)
    cot_f32 = cotangent.astype(jnp.float32)
    grad_rows = (route_scale * cot_f32[:, None, :]).astype(jnp.bfloat16)
    grad_sent = jnp.einsum(
        "tks,tkd->sd", route_table, grad_rows, preferred_element_type=jnp.float32
    ).astype(jnp.bfloat16)
    grad_expert = over_experts(grad_sent.reshape(ctx_count, capacity, model_width)).reshape(
        -1, model_width
    )
    grad_act = jnp.dot(grad_expert, w_down[0].T, preferred_element_type=jnp.float32)
    grad_gate_pre = (
        grad_act * (up_pre + 1.0) * (gate_sig + GLU_ALPHA * gate_glu * (1.0 - gate_sig))
    ).astype(jnp.bfloat16)
    grad_up_pre = (grad_act * gate_glu).astype(jnp.bfloat16)
    grad_down = jnp.dot(activated.T, grad_expert, preferred_element_type=jnp.float32).astype(
        jnp.bfloat16
    )[None]
    grad_gate = jnp.dot(expert_rows.T, grad_gate_pre, preferred_element_type=jnp.float32).astype(
        jnp.bfloat16
    )[None]
    grad_up = jnp.dot(expert_rows.T, grad_up_pre, preferred_element_type=jnp.float32).astype(
        jnp.bfloat16
    )[None]
    input_part = jnp.dot(grad_gate_pre, w_gate[0].T, preferred_element_type=jnp.float32) + jnp.dot(
        grad_up_pre, w_up[0].T, preferred_element_type=jnp.float32
    )
    input_part = input_part.astype(jnp.bfloat16).reshape(ctx_count, capacity, model_width)
    grad_returned = back_from_experts(input_part)
    grad_normed = sum_heads(jnp.sum(pick_rows(grad_returned, route_table), axis=1))
    grad_resid = cot_f32 + rms_back(residual_f32, resid_scale, grad_normed)
    grad_resid_bf = grad_resid.astype(jnp.bfloat16)
    attended_gradient = jnp.dot(
        grad_resid_bf, full_output.T, preferred_element_type=jnp.float32
    ).astype(jnp.bfloat16)
    query_gradients, key_value_gradients = attention_backward(
        query_heads,
        banded_key_span,
        probability_single,
        probability_half,
        attended_gradient.reshape(row_count, kv_heads, query_head_group, HEAD_SIZE),
    )
    rim_grad = shifted(key_value_gradients[:WINDOW].astype(jnp.bfloat16), "ctx", -1).astype(
        jnp.float32
    )
    local_gradient = key_value_gradients[WINDOW:].at[row_count - WINDOW :].add(rim_grad)
    key_value_grad = local_gradient.reshape(row_count, -1).astype(jnp.bfloat16)
    query_grad = query_gradients.reshape(row_count, -1).astype(jnp.bfloat16)
    grad_normed_in = sum_heads(
        jnp.dot(query_grad, full_query.T, preferred_element_type=jnp.float32)
        + jnp.dot(key_value_grad, full_keyval.T, preferred_element_type=jnp.float32)
    )
    grad_tokens = (grad_resid + rms_back(tokens_f32, token_scale, grad_normed_in)).astype(
        jnp.bfloat16
    )
    terms = (
        rounded(jnp.dot(normed.T, query_grad, preferred_element_type=jnp.float32)),
        rounded(jnp.dot(normed.T, key_value_grad, preferred_element_type=jnp.float32)),
        rounded(jnp.dot(attended_flat.T, grad_resid_bf, preferred_element_type=jnp.float32)),
    )
    sum_query, sum_keyval, sum_output = (
        lax.psum_scatter(
            terms[0].astype(jnp.bfloat16), "ctx", scatter_dimension=0, tiled=True
        ).astype(jnp.float32),
        lax.psum_scatter(
            terms[1].astype(jnp.bfloat16), "ctx", scatter_dimension=0, tiled=True
        ).astype(jnp.float32),
        lax.psum_scatter(
            terms[2].astype(jnp.bfloat16), "ctx", scatter_dimension=1, tiled=True
        ).astype(jnp.float32),
    )
    return (
        block_out,
        grad_tokens,
        sum_query.astype(jnp.bfloat16),
        sum_keyval.astype(jnp.bfloat16),
        sum_output.astype(jnp.bfloat16),
        grad_gate,
        grad_up,
        grad_down,
    )


def solution(mesh):
    in_specs = (
        P("ctx", None),
        P("ctx", None),
        P("ctx", None),
        P("ctx", None),
        P("ctx", "exp"),
        P("ctx", "exp"),
        P("exp", "ctx"),
        P("ctx", None, "exp"),
        P("ctx", None, "exp"),
        P("ctx", "exp", None),
    )
    out_specs = (
        P("ctx", None),
        P("ctx", None),
        P("ctx", "exp"),
        P("ctx", "exp"),
        P("exp", "ctx"),
        P("ctx", None, "exp"),
        P("ctx", None, "exp"),
        P("ctx", "exp", None),
    )
    return jax.shard_map(body, mesh=mesh, in_specs=in_specs, out_specs=out_specs, check_vma=False)
```

profile of v0, /device:TPU:82, one launch (start us, length us, event | category | flops | bytes accessed | tf_op | source)
XLA Modules:
  0.0 897.1 jit_solution(17111580672626592761)
XLA Ops:
  11.9 4.1 bitcast_convert_fusion
  16.1 6.2 copy.78
  22.2 6.5 reshape.269
  28.7 8.9 all-to-all-start.2
  38.5 124.4 %all-gather = bf16[32,90,128]{2,1,0:T(8,128)(2,1)} all-gather(bf16[1,90,128]{2,1,0:T(8,128)(2,1)S(1)} %bitcast.179), channel_id=1, replica_groups=mesh['ctx'=32,'exp'=8] {'ctx'}, dimensions={0}, use_global_device_ids=true | all-gather | bytes 760320 | tf_op jit(solution)/shard_map/all_gather | solution.py:127
  165.6 4.1 collective-permute-start
  169.9 2.4 collective-permute-done
  172.5 10.1 %all-gather.6.cloned.1.call-done = bf16[32,90,256]{2,1,0:T(8,128)(2,1)} async-done(((bf16[1,90,256]{2,1,0:T(8,128)(2,1)}), bf16[32,90,256]{2,1,0:T(8,128)(2,1)}) %all-gather.6.cloned.1.call-update) | async-done | bytes 1474576 | tf_op jit(solution)/shard_map/all_gather | solution.py:126
  182.5 3.4 reshape.278
  187.8 150.4 %all-gather.8.cloned.1.call-done = bf16[32,90,256]{2,1,0:T(8,128)(2,1)} async-done(((bf16[1,90,256]{2,1,0:T(8,128)(2,1)}), bf16[32,90,256]{2,1,0:T(8,128)(2,1)}) %all-gather.8.cloned.1.call-update) | async-done | bytes 1474576 | tf_op jit(solution)/shard_map/all_gather | solution.py:128
  338.2 3.4 reshape.280
  344.8 81.4 %all-reduce.12.cloned.1.call-done = bf16[128,2880]{0,1:T(8,128)(2,1)} async-done(((bf16[128,2880]{0,1:T(8,128)(2,1)}), bf16[128,2880]{0,1:T(8,128)(2,1)}) %all-reduce.12.cloned.1.call-update) | async-done | bytes 737296 | tf_op jit(solution)/shard_map/psum | solution.py:92
  427.7 3.0 convolution_convert_fusion
  430.7 6.2 copy.75
  436.9 6.5 reshape.265
  443.4 7.4 all-to-all-start
  450.8 6.5 reshape.270
  457.3 51.7 %all-to-all-done = bf16[32,20,2880]{2,1,0:T(8,128)(2,1)} async-done(((bf16[32,20,2880]{2,1,0:T(8,128)(2,1)}), bf16[32,20,2880]{2,1,0:T(8,128)(2,1)}, u32[]{:S(2)}, u32[]{:S(2)}) %all-to-all-start) | async-done | bytes 3686432 | tf_op jit(solution)/shard_map/all_to_all | solution.py:96
  509.1 6.4 reshape.266
  515.5 3.8 fusion.46
  524.7 3.2 add_convert_fusion
  527.9 6.2 copy.79
  534.1 6.5 reshape.271
  540.6 10.1 %all-to-all-start.3 = ((bf16[32,20,2880]{2,1,0:T(8,128)(2,1)}), bf16[32,20,2880]{2,1,0:T(8,128)(2,1)}, u32[]{:S(2)}, u32[]{:S(2)}) async-start(bf16[32,20,2880]{2,1,0:T(8,128)(2,1)} %reshape.271), calls=%async_computation.3 | async-start | bytes 9043968 | tf_op jit(solution)/shard_map/all_to_all | solution.py:100
  550.7 3.2 convolution_convert_fusion.1
  553.8 6.2 copy.76
  560.1 6.4 reshape.267
  566.5 52.8 %all-to-all-done.3 = bf16[32,20,2880]{2,1,0:T(8,128)(2,1)} async-done(((bf16[32,20,2880]{2,1,0:T(8,128)(2,1)}), bf16[32,20,2880]{2,1,0:T(8,128)(2,1)}, u32[]{:S(2)}, u32[]{:S(2)}) %all-to-all-start.3) | async-done | bytes 3686432 | tf_op jit(solution)/shard_map/all_to_all | solution.py:100
  619.3 9.3 %all-to-all-start.1 = ((bf16[32,20,2880]{2,1,0:T(8,128)(2,1)}), bf16[32,20,2880]{2,1,0:T(8,128)(2,1)}, u32[]{:S(2)}, u32[]{:S(2)}) async-start(bf16[32,20,2880]{2,1,0:T(8,128)(2,1)} %reshape.267), calls=%async_computation.1 | async-start | bytes 9043968 | tf_op jit(solution)/shard_map/all_to_all | solution.py:100
  630.1 4.6 fusion.7
  634.7 6.5 reshape.272
  641.2 6.6 fusion.12
  648.0 4.6 fusion.6
  652.5 38.2 %all-to-all-done.1 = bf16[32,20,2880]{2,1,0:T(8,128)(2,1)} async-done(((bf16[32,20,2880]{2,1,0:T(8,128)(2,1)}), bf16[32,20,2880]{2,1,0:T(8,128)(2,1)}, u32[]{:S(2)}, u32[]{:S(2)}) %all-to-all-start.1) | async-done | bytes 3686432 | tf_op jit(solution)/shard_map/all_to_all | solution.py:100
  690.7 6.5 reshape.268
  697.2 6.7 multiply_reduce_fusion
  704.0 18.5 %all-reduce.14.cloned.1.call-done = bf16[128,2880]{0,1:T(8,128)(2,1)} async-done(((bf16[128,2880]{0,1:T(8,128)(2,1)}), bf16[128,2880]{0,1:T(8,128)(2,1)}) %all-reduce.14.cloned.1.call-update) | async-done | bytes 737296 | tf_op jit(solution)/shard_map/psum | solution.py:92
  724.6 2.8 convolution_convert_fusion.10
  730.8 2.5 collective-permute-start.1
  739.1 95.0 %fusion.78 = (bf16[96,256]{1,0:T(8,128)(2,1)S(1)}, bf16[96,128]{1,0:T(8,128)(2,1)S(1)}, bf16[256,96]{0,1:T(8,128)(2,1)S(1)}) fusion(bf16[2880,256]{1,0:T(8,128)(2,1)S(1)} %convolution_convert_fusion.6, bf16[2880,128]{1,0:T(8,128)(2,1)} %convolution_convert_fusion.7, bf16[256,2880]{0,1:T(8,128)(2,1)} %convolution_convert_fusion.5), kind=kCustom, calls=%all-reduce-scatter.3 | all-reduce-scatter fusion | flops 1966081 | bytes 3810304
  834.1 4.3 collective-permute-start.4
  838.4 11.3 %collective-permute-start.5 = (bf16[90,128]{1,0:T(8,128)(2,1)S(1)}, bf16[90,128]{1,0:T(8,128)(2,1)S(1)}, u32[]{:S(2)}, u32[]{:S(2)}) collective-permute-start(bf16[90,128]{1,0:T(8,128)(2,1)S(1)} %slice.57), channel_id=1, source_target_pairs={{0,16},{8,24},{16,32},{24,40},{32,48},{40,56},{48,64},{56,72},{64,... | collective-permute-start | bytes 69128
  849.8 4.8 fusion.8
  854.6 3.4 collective-permute-start.2
  858.1 5.4 collective-permute-start.6
  863.5 11.3 %collective-permute-start.7 = (bf16[256,90]{0,1:T(8,128)(2,1)S(1)}, bf16[256,90]{0,1:T(8,128)(2,1)S(1)}, u32[]{:S(2)}, u32[]{:S(2)}) collective-permute-start(bf16[256,90]{0,1:T(8,128)(2,1)S(1)} %slice.58), channel_id=1, source_target_pairs={{0,16},{8,24},{16,32},{24,40},{32,48},{40,56},{48,64},{56,72},{64,... | collective-permute-start | bytes 138248
  877.8 5.4 collective-permute-done.3
  887.1 3.5 fusion.19
  (154 shorter events, 39.4 us)
Async XLA Ops:
  7.2 513.6 %copy-start = (bf16[1,256,2880]{1,2,0:T(8,128)(2,1)S(1)}, bf16[1,256,2880]{1,2,0:T(8,128)(2,1)}, u32[]{:S(2)}) copy-start(bf16[1,256,2880]{1,2,0:T(8,128)(2,1)} %param.23) | copy-start | bytes 4423684
  7.2 175.3 %all-gather.6.cloned.1.call-start = ((), (), s32[]{:S(2)}) async-start(), calls=%async_computation.6 | async-start | bytes 1622016 | tf_op jit(solution)/shard_map/all_gather | solution.py:126
  7.2 4.7 copy-start.31
  7.2 4.7 copy-start.36
  28.7 9.7 %copy-start.30 = (bf16[90,128]{1,0:T(8,128)(2,1)S(1)}, bf16[90,128]{1,0:T(8,128)(2,1)}, u32[]{:S(2)}) copy-start(bf16[90,128]{1,0:T(8,128)(2,1)} %param.19) | copy-start | bytes 69124
  28.7 414.7 %all-to-all-start.2 = ((bf16[32,20,2880]{2,1,0:T(8,128)(2,1)}), bf16[32,20,2880]{2,1,0:T(8,128)(2,1)}, u32[]{:S(2)}, u32[]{:S(2)}) async-start(bf16[32,20,2880]{2,1,0:T(8,128)(2,1)} %reshape.269), calls=%async_computation.2 | async-start | bytes 9043968 | tf_op jit(solution)/shard_map/all_to_all | solution.py:96
  37.6 126.6 %copy-start.2 = (bf16[128,2880]{0,1:T(8,128)(2,1)S(1)}, bf16[128,2880]{0,1:T(8,128)(2,1)}, u32[]{:S(2)}) copy-start(bf16[128,2880]{0,1:T(8,128)(2,1)} %param.14) | copy-start | bytes 2211844
  37.6 300.6 %all-gather.8.cloned.1.call-start = ((), (), s32[]{:S(2)}) async-start(), calls=%async_computation.7 | async-start | bytes 1622016 | tf_op jit(solution)/shard_map/all_gather | solution.py:128
  38.4 387.8 %all-reduce.12.cloned.1.call-start = ((), (), s32[]{:S(2)}) async-start(), calls=%async_computation.4 | async-start | bytes 1474560 | tf_op jit(solution)/shard_map/psum | solution.py:92
  164.2 21.6 %copy-start.12 = (bf16[2880,128]{1,0:T(8,128)(2,1)}, bf16[2880,128]{1,0:T(8,128)(2,1)S(1)}, u32[]{:S(2)}) copy-start(bf16[2880,128]{1,0:T(8,128)(2,1)S(1)} %reshape.276) | copy-start | bytes 2211844
  165.6 6.7 collective-permute-start
  172.4 169.4 %copy-start.27 = (bf16[256,128]{0,1:T(8,128)(2,1)}, bf16[256,128]{0,1:T(8,128)(2,1)S(1)}, u32[]{:S(2)}) copy-start(bf16[256,128]{0,1:T(8,128)(2,1)S(1)} %copy.68) | copy-start | bytes 196612
  187.8 153.8 %copy-start.25 = (bf16[128,256]{0,1:T(8,128)(2,1)}, bf16[128,256]{0,1:T(8,128)(2,1)S(1)}, u32[]{:S(2)}) copy-start(bf16[128,256]{0,1:T(8,128)(2,1)S(1)} %copy.69) | copy-start | bytes 196612
  341.6 1.6 copy-start.8
  341.9 2.7 copy-start.17
  443.4 65.7 %all-to-all-start = ((bf16[32,20,2880]{2,1,0:T(8,128)(2,1)}), bf16[32,20,2880]{2,1,0:T(8,128)(2,1)}, u32[]{:S(2)}, u32[]{:S(2)}) async-start(bf16[32,20,2880]{2,1,0:T(8,128)(2,1)} %reshape.265), calls=%async_computation | async-start | bytes 9043968 | tf_op jit(solution)/shard_map/all_to_all | solution.py:96
  515.5 3.8 copy-start.10
  515.5 4.1 copy-start.14
  519.6 2.1 copy-start.9
  523.0 1.4 copy-start.23
  523.0 27.7 %copy-start.19 = (bf16[640,256]{1,0:T(8,128)(2,1)}, bf16[640,256]{1,0:T(8,128)(2,1)S(1)}, u32[]{:S(2)}) copy-start(bf16[640,256]{1,0:T(8,128)(2,1)S(1)} %get-tuple-element.40) | copy-start | bytes 983044
  523.0 1.7 copy-start.15
  540.6 78.8 %all-to-all-start.3 = ((bf16[32,20,2880]{2,1,0:T(8,128)(2,1)}), bf16[32,20,2880]{2,1,0:T(8,128)(2,1)}, u32[]{:S(2)}, u32[]{:S(2)}) async-start(bf16[32,20,2880]{2,1,0:T(8,128)(2,1)} %reshape.271), calls=%async_computation.3 | async-start | bytes 9043968 | tf_op jit(solution)/shard_map/all_to_all | solution.py:100
  566.5 62.4 %copy-start.35 = (u32[256]{0:T(256)S(1)}, u32[256]{0:T(256)}, u32[]{:S(2)}) copy-start(u32[256]{0:T(256)} %constant.82) | copy-start | bytes 3076
  566.5 63.6 %copy-start.22 = (bf16[640,256]{1,0:T(8,128)(2,1)S(1)}, bf16[640,256]{1,0:T(8,128)(2,1)}, u32[]{:S(2)}) copy-start(bf16[640,256]{1,0:T(8,128)(2,1)} %copy-done.21) | copy-start | bytes 983044
  619.3 71.4 %all-to-all-start.1 = ((bf16[32,20,2880]{2,1,0:T(8,128)(2,1)}), bf16[32,20,2880]{2,1,0:T(8,128)(2,1)}, u32[]{:S(2)}, u32[]{:S(2)}) async-start(bf16[32,20,2880]{2,1,0:T(8,128)(2,1)} %reshape.267), calls=%async_computation.1 | async-start | bytes 9043968 | tf_op jit(solution)/shard_map/all_to_all | solution.py:100
  628.6 93.9 %all-reduce.14.cloned.1.call-start = ((), (), s32[]{:S(2)}) async-start(), calls=%async_computation.5 | async-start | bytes 1474560 | tf_op jit(solution)/shard_map/psum | solution.py:92
  641.2 6.7 copy-start.24
  647.9 237.5 %all-reduce.16.cloned.1.call-start = ((), (), s32[]{:S(2)}) async-start(), calls=%async_computation.8 | async-start | bytes 2949120 | tf_op jit(solution)/shard_map/psum | solution.py:92
  704.0 20.6 %copy-start.4 = (bf16[128,2880]{0,1:T(8,128)(2,1)S(1)}, bf16[128,2880]{0,1:T(8,128)(2,1)}, u32[]{:S(2)}) copy-start(bf16[128,2880]{0,1:T(8,128)(2,1)} %param.15) | copy-start | bytes 2211844
  722.5 2.1 copy-start.6
  724.6 3.8 copy-start.18
  730.2 3.0 copy-start.5
  730.2 3.0 copy-start.7
  730.2 3.0 copy-start.33
  730.8 5.8 collective-permute-start.1
  735.0 2.8 copy-start.13
  739.1 110.7 %copy-start.20 = (bf16[640,256]{1,0:T(8,128)(2,1)S(1)}, bf16[640,256]{1,0:T(8,128)(2,1)}, u32[]{:S(2)}) copy-start(bf16[640,256]{1,0:T(8,128)(2,1)} %copy-done.19) | copy-start | bytes 983044
  834.1 42.6 %collective-permute-start.4 = (bf16[96,128]{1,0:T(8,128)(2,1)S(1)}, bf16[96,128]{1,0:T(8,128)(2,1)S(1)}, u32[]{:S(2)}, u32[]{:S(2)}) collective-permute-start(bf16[96,128]{1,0:T(8,128)(2,1)S(1)} %get-tuple-element.34), channel_id=1, source_target_pairs={{0,8},{8,16},{16,24},{24,32},{32,40},{40,48},{48,56},{56,64},{64,7... | collective-permute-start | bytes 73736
  838.4 36.4 %collective-permute-start.5 = (bf16[90,128]{1,0:T(8,128)(2,1)S(1)}, bf16[90,128]{1,0:T(8,128)(2,1)S(1)}, u32[]{:S(2)}, u32[]{:S(2)}) collective-permute-start(bf16[90,128]{1,0:T(8,128)(2,1)S(1)} %slice.57), channel_id=1, source_target_pairs={{0,16},{8,24},{16,32},{24,40},{32,48},{40,56},{48,64},{56,72},{64,... | collective-permute-start | bytes 69128
  854.6 32.5 %copy-start.34 = (f32[128]{0:T(128)S(1)}, f32[128]{0:T(128)}, u32[]{:S(2)}) copy-start(f32[128]{0:T(128)} %get-tuple-element.43) | copy-start | bytes 1540
  854.6 28.6 %collective-permute-start.2 = (bf16[96,256]{1,0:T(8,128)(2,1)S(1)}, bf16[96,256]{1,0:T(8,128)(2,1)S(1)}, u32[]{:S(2)}, u32[]{:S(2)}) collective-permute-start(bf16[96,256]{1,0:T(8,128)(2,1)S(1)} %get-tuple-element.33), channel_id=1, source_target_pairs={{0,8},{8,16},{16,24},{24,32},{32,40},{40,48},{48,56},{56,64},{64,7... | collective-permute-start | bytes 147464
  858.1 25.6 %collective-permute-start.6 = (bf16[256,96]{0,1:T(8,128)(2,1)S(1)}, bf16[256,96]{0,1:T(8,128)(2,1)S(1)}, u32[]{:S(2)}, u32[]{:S(2)}) collective-permute-start(bf16[256,96]{0,1:T(8,128)(2,1)S(1)} %get-tuple-element.35), channel_id=1, source_target_pairs={{0,8},{8,16},{16,24},{24,32},{32,40},{40,48},{48,56},{56,64},{64,7... | collective-permute-start | bytes 147464
  863.5 20.2 %collective-permute-start.7 = (bf16[256,90]{0,1:T(8,128)(2,1)S(1)}, bf16[256,90]{0,1:T(8,128)(2,1)S(1)}, u32[]{:S(2)}, u32[]{:S(2)}) collective-permute-start(bf16[256,90]{0,1:T(8,128)(2,1)S(1)} %slice.58), channel_id=1, source_target_pairs={{0,16},{8,24},{16,32},{24,40},{32,48},{40,56},{48,64},{56,72},{64,... | collective-permute-start | bytes 138248
  874.8 8.4 collective-permute-start.3
  885.4 1.6 copy-start.11
  885.4 1.6 copy-start.16
  887.1 3.5 copy-start.1
  (6 other events, 6.4 us)
Sparse Core Ops, SparseCore 0:
  9.8 172.6 all-gather.5
  184.3 153.8 all-gather.7
  344.7 81.4 all-reduce.11
  648.0 74.3 all-reduce.13
  739.2 84.5 all-reduce.15
where the time goes:
time: 900 us; the launch traced here: 897 us
  waiting for transfers between devices  413 us (46%)
  blocking collectives  219 us (24%)
  local copies, waits for them, and re-layouts  95.2 us (11%)
  starting transfers between devices  80.3 us (9%)
  matrix products  61.4 us (7%)
  between operations  15.1 us (2%)
  other arithmetic  12.2 us (1%)
    all_gather x1, waiting for transfers between devices, body(): lax.all_gather(w_output, 'ctx', axis=1, tiled=True)  150 us
    all_gather x1, blocking collectives, body(): lax.all_gather(key_value_weight, 'ctx', axis=0, tiled=True)  124 us
    psum x3, waiting for transfers between devices, sum_heads(): return lax.psum(values.astype(jnp.bfloat16), 'exp').astype(jnp.float32)  99.9 us
    unnamed x1, blocking collectives  95 us
    all_to_all x2, waiting for transfers between devices, back_from_experts(): lax.all_to_all(buffer, 'ctx', split_axis=0, concat_axis=0, tiled=True)  91 us
    all_to_all x2, waiting for transfers between devices, over_experts(): lax.all_to_all(buffer, 'ctx', split_axis=0, concat_axis=0, tiled=True)  51.7 us
    unnamed x6, starting transfers between devices  37.7 us
    all_to_all x2, starting transfers between devices, back_from_experts(): lax.all_to_all(buffer, 'ctx', split_axis=0, concat_axis=0, tiled=True)  19.3 us
  transfers between devices with their start and end apart: 17, of which 10 were waited for; matrix products, arithmetic and copies ran while one was open for 24% of the time, Pallas kernels for 0%

commit v1 on v0

--- a/solution.py
+++ b/solution.py
@@ -89,7 +89,12 @@
 
 
 def sum_heads(values):
-    return lax.psum(values.astype(jnp.bfloat16), "exp").astype(jnp.float32)
+
+    def lift_the_surface(shard_in):
+        wide_out = lax.all_gather(shard_in, axis_name="exp").sum(axis=0)
+        return wide_out
+
+    return lift_the_surface(values.astype(jnp.bfloat16)).astype(jnp.float32)
 
 
 def over_experts(buffer):

time: 900 us -> 1050 us (1.17)
  blocking collectives: 219 us -> 349 us
  other arithmetic: 12.2 us -> 57.8 us
  waiting for transfers between devices: 413 us -> 381 us
  local copies, waits for them, and re-layouts: 95.2 us -> 113 us
  starting transfers between devices: 80.3 us -> 66.9 us
    all_to_all x0 -> x2, blocking collectives: none -> 156 us  [back_from_experts(): lax.all_to_all(buffer, 'ctx', split_axis=0, concat_axis=0, tiled=True)]
    psum x3 -> x0, waiting for transfers between devices: 99.9 us -> none  [sum_heads(): return lax.psum(values.astype(jnp.bfloat16), 'exp').astype(jnp.float32)]
    all_gather x0 -> x4, waiting for transfers between devices: none -> 98.8 us  [lift_the_surface(): wide_out = lax.all_gather(shard_in, axis_name='exp').sum(axis=0)]
    all_to_all x2 -> x0, waiting for transfers between devices: 91 us -> none  [back_from_experts(): lax.all_to_all(buffer, 'ctx', split_axis=0, concat_axis=0, tiled=True)]
    all_gather x1, waiting for transfers between devices: 10.1 us -> 66.5 us  [body(): lax.all_gather(w_query, 'ctx', axis=0, tiled=True)]
    reduce_sum x0 -> x4, other arithmetic: none -> 51.6 us  [lift_the_surface(): wide_out = lax.all_gather(shard_in, axis_name='exp').sum(axis=0)]
    all_gather x1, blocking collectives: 124 us -> 74.2 us  [body(): lax.all_gather(key_value_weight, 'ctx', axis=0, tiled=True)]
    unnamed x1, blocking collectives: 95 us -> 119 us
  transfers between devices with their start and end apart: 17 -> 16, of which waited for: 10 -> 8; matrix products, arithmetic and copies ran while one was open for 24% -> 27% of each run, Pallas kernels for 0% -> 0%
where the time goes in v1:
time: 1050 us; the launch traced here: 1040 us
  waiting for transfers between devices  381 us (36%)
  blocking collectives  349 us (33%)
  local copies, waits for them, and re-layouts  113 us (11%)
  starting transfers between devices  66.9 us (6%)
  matrix products  59.1 us (6%)
  other arithmetic  57.8 us (6%)
  between operations  16 us (2%)
    all_to_all x2, blocking collectives, back_from_experts(): lax.all_to_all(buffer, 'ctx', split_axis=0, concat_axis=0, tiled=True)  156 us
    all_gather x1, waiting for transfers between devices, body(): lax.all_gather(w_output, 'ctx', axis=1, tiled=True)  151 us
    unnamed x1, blocking collectives  119 us
    all_gather x4, waiting for transfers between devices, lift_the_surface(): wide_out = lax.all_gather(shard_in, axis_name='exp').sum(axis=0)  98.8 us
    all_gather x1, blocking collectives, body(): lax.all_gather(key_value_weight, 'ctx', axis=0, tiled=True)  74.2 us
    all_gather x1, waiting for transfers between devices, body(): lax.all_gather(w_query, 'ctx', axis=0, tiled=True)  66.5 us
    all_to_all x2, waiting for transfers between devices, over_experts(): lax.all_to_all(buffer, 'ctx', split_axis=0, concat_axis=0, tiled=True)  55.1 us
    reduce_sum x4, other arithmetic, lift_the_surface(): wide_out = lax.all_gather(shard_in, axis_name='exp').sum(axis=0)  51.6 us
  transfers between devices with their start and end apart: 16, of which 8 were waited for; matrix products, arithmetic and copies ran while one was open for 27% of the time, Pallas kernels for 0%

profile of v1, /device:TPU:82, one launch (start us, length us, event | category | flops | bytes accessed | tf_op | source)
XLA Modules:
  0.0 1043.2 jit_solution(212107295934894280)
XLA Ops:
  8.7 74.2 %all-gather.4 = bf16[32,90,128]{2,1,0:T(8,128)(2,1)} all-gather(bf16[1,90,128]{2,1,0:T(8,128)(2,1)} %bitcast.203), channel_id=1, replica_groups=mesh['ctx'=32,'exp'=8] {'ctx'}, dimensions={0}, use_global_device_ids=true | all-gather | bytes 760320 | tf_op jit(solution)/shard_map/all_gather | solution.py:132
  85.7 4.5 collective-permute-start
  91.9 66.5 %all-gather.22.cloned.1.call-done = bf16[32,90,256]{2,1,0:T(8,128)(2,1)} async-done(((bf16[1,90,256]{2,1,0:T(8,128)(2,1)}), bf16[32,90,256]{2,1,0:T(8,128)(2,1)}) %all-gather.22.cloned.1.call-update) | async-done | bytes 1474576 | tf_op jit(solution)/shard_map/all_gather | solution.py:131
  158.3 3.4 reshape.298
  164.1 151.2 %all-gather.24.cloned.1.call-done = bf16[32,90,256]{2,1,0:T(8,128)(2,1)} async-done(((bf16[1,90,256]{2,1,0:T(8,128)(2,1)}), bf16[32,90,256]{2,1,0:T(8,128)(2,1)}) %all-gather.24.cloned.1.call-update) | async-done | bytes 1474576 | tf_op jit(solution)/shard_map/all_gather | solution.py:133
  315.3 3.4 reshape.300
  318.7 2.9 convolution_convert_fusion.8
  323.8 4.2 bitcast_convert_fusion
  328.0 6.2 copy.78
  334.2 6.4 reshape.285
  340.6 16.4 %all-to-all-start.2 = ((bf16[32,20,2880]{2,1,0:T(8,128)(2,1)}), bf16[32,20,2880]{2,1,0:T(8,128)(2,1)}, u32[]{:S(2)}, u32[]{:S(2)}) async-start(bf16[32,20,2880]{2,1,0:T(8,128)(2,1)} %reshape.285), calls=%async_computation.2 | async-start | bytes 9043968 | tf_op jit(solution)/shard_map/all_to_all | solution.py:101
  357.3 68.4 %all-gather.14.cloned.1.call-done = bf16[1024,2880]{0,1:T(8,128)(2,1)} async-done(((bf16[128,2880]{0,1:T(8,128)(2,1)}), bf16[1024,2880]{0,1:T(8,128)(2,1)}) %all-gather.14.cloned.1.call-update) | async-done | bytes 5898256 | tf_op jit(solution)/shard_map/all_gather | solution.py:94
  425.7 4.2 copy.94
  429.9 12.3 %bitcast_reduce_fusion.3 = bf16[128,2880]{0,1:T(8,128)(2,1)S(1)} fusion(bf16[360,8,8,128]{3,2,1,0:T(8,128)(2,1)S(1)} %copy.94), kind=kLoop, calls=%fused_computation.5 | loop fusion | flops 2580480 | bytes 6635520 | tf_op jit(solution)/shard_map/reduce_sum | solution.py:94
  442.6 2.9 convolution_convert_fusion
  445.5 6.2 copy.75
  451.6 6.4 reshape.281
  458.1 7.4 all-to-all-start
  466.0 6.5 reshape.286
  472.5 55.1 %all-to-all-done = bf16[32,20,2880]{2,1,0:T(8,128)(2,1)} async-done(((bf16[32,20,2880]{2,1,0:T(8,128)(2,1)}), bf16[32,20,2880]{2,1,0:T(8,128)(2,1)}, u32[]{:S(2)}, u32[]{:S(2)}) %all-to-all-start) | async-done | bytes 3686432 | tf_op jit(solution)/shard_map/all_to_all | solution.py:101
  527.6 6.5 reshape.282
  534.1 3.8 fusion.46
  543.3 3.1 add_convert_fusion
  546.4 6.2 copy.79
  552.7 6.4 reshape.287
  559.1 59.9 %all_to_all.20 = bf16[32,20,2880]{2,1,0:T(8,128)(2,1)} all-to-all(bf16[32,20,2880]{2,1,0:T(8,128)(2,1)} %reshape.287), channel_id=1, replica_groups=mesh['ctx'=32,'exp'=8] {'ctx'}, dimensions={0} | all-to-all | bytes 7372800 | tf_op jit(solution)/shard_map/all_to_all | solution.py:105
  619.0 6.5 reshape.288
  625.4 6.6 fusion.12
  632.2 3.1 convolution_convert_fusion.1
  635.3 6.2 copy.76
  641.5 6.5 reshape.283
  647.9 96.4 %all_to_all.21 = bf16[32,20,2880]{2,1,0:T(8,128)(2,1)} all-to-all(bf16[32,20,2880]{2,1,0:T(8,128)(2,1)} %reshape.283), channel_id=1, replica_groups=mesh['ctx'=32,'exp'=8] {'ctx'}, dimensions={0} | all-to-all | bytes 7372800 | tf_op jit(solution)/shard_map/all_to_all | solution.py:105
  744.4 6.5 reshape.284
  750.9 6.7 multiply_reduce_fusion
  757.7 4.2 copy.96
  761.9 12.3 %bitcast_reduce_fusion.1 = bf16[128,2880]{0,1:T(8,128)(2,1)S(1)} fusion(bf16[360,8,8,128]{3,2,1,0:T(8,128)(2,1)S(1)} %copy.96), kind=kLoop, calls=%fused_computation.3 | loop fusion | flops 2580480 | bytes 6635520 | tf_op jit(solution)/shard_map/reduce_sum | solution.py:94
  780.5 3.6 collective-permute-start.1
  788.9 5.0 fusion.8
  798.9 30.4 %all-gather.16.cloned.1.call-done = bf16[1024,2880]{0,1:T(8,128)(2,1)} async-done(((bf16[128,2880]{0,1:T(8,128)(2,1)}), bf16[1024,2880]{0,1:T(8,128)(2,1)}) %all-gather.16.cloned.1.call-update) | async-done | bytes 5898256 | tf_op jit(solution)/shard_map/all_gather | solution.py:94
  829.3 6.8 copy.95
  839.6 118.6 %fusion.78 = (bf16[96,256]{1,0:T(8,128)(2,1)S(1)}, bf16[96,128]{1,0:T(8,128)(2,1)S(1)}, bf16[256,96]{0,1:T(8,128)(2,1)S(1)}) fusion(bf16[2880,256]{1,0:T(8,128)(2,1)S(1)} %convolution_convert_fusion.6, bf16[2880,128]{1,0:T(8,128)(2,1)} %convolution_convert_fusion.7, bf16[256,2880]{0,1:T(8,128)(2,1)} %convolution_convert_fusion.5), kind=kCustom, calls=%all-reduce-scatter.3 | all-reduce-scatter fusion | flops 1966081 | bytes 3810304
  961.0 10.2 collective-permute-start.5
  971.2 14.7 %bitcast_reduce_fusion.2 = bf16[128,2880]{0,1:T(8,128)(2,1)} fusion(bf16[360,8,8,128]{3,2,1,0:T(8,128)(2,1)} %copy.95), kind=kLoop, calls=%fused_computation.4 | loop fusion | flops 2580480 | bytes 6635520 | tf_op jit(solution)/shard_map/reduce_sum | solution.py:94
  988.7 4.9 collective-permute-start.6
  993.7 11.8 %collective-permute-start.7 = (bf16[256,90]{0,1:T(8,128)(2,1)S(1)}, bf16[256,90]{0,1:T(8,128)(2,1)S(1)}, u32[]{:S(2)}, u32[]{:S(2)}) collective-permute-start(bf16[256,90]{0,1:T(8,128)(2,1)S(1)} %slice.58), channel_id=1, source_target_pairs={{0,16},{8,24},{16,32},{24,40},{32,48},{40,56},{48,64},{56,72},{64,... | collective-permute-start | bytes 138248
  1008.5 5.4 collective-permute-done.3
  1016.1 4.2 copy.97
  1020.3 12.3 %bitcast_reduce_fusion = bf16[128,2880]{0,1:T(8,128)(2,1)S(1)} fusion(bf16[360,8,8,128]{3,2,1,0:T(8,128)(2,1)S(1)} %copy.97), kind=kLoop, calls=%fused_computation.2 | loop fusion | flops 2580480 | bytes 6635520 | tf_op jit(solution)/shard_map/reduce_sum | solution.py:94
  (167 shorter events, 49.7 us)
Async XLA Ops:
  7.2 532.2 %copy-start = (bf16[1,256,2880]{1,2,0:T(8,128)(2,1)S(1)}, bf16[1,256,2880]{1,2,0:T(8,128)(2,1)}, u32[]{:S(2)}) copy-start(bf16[1,256,2880]{1,2,0:T(8,128)(2,1)} %param.23) | copy-start | bytes 4423684
  7.2 77.1 %copy-start.2 = (bf16[128,2880]{0,1:T(8,128)(2,1)S(1)}, bf16[128,2880]{0,1:T(8,128)(2,1)}, u32[]{:S(2)}) copy-start(bf16[128,2880]{0,1:T(8,128)(2,1)} %param.14) | copy-start | bytes 2211844
  7.2 151.1 %all-gather.22.cloned.1.call-start = ((), (), s32[]{:S(2)}) async-start(), calls=%async_computation.8 | async-start | bytes 1622016 | tf_op jit(solution)/shard_map/all_gather | solution.py:131
  7.9 307.4 %all-gather.24.cloned.1.call-start = ((), (), s32[]{:S(2)}) async-start(), calls=%async_computation.9 | async-start | bytes 1622016 | tf_op jit(solution)/shard_map/all_gather | solution.py:133
  8.7 417.0 %all-gather.14.cloned.1.call-start = ((), (), s32[]{:S(2)}) async-start(), calls=%async_computation.4 | async-start | bytes 6635520 | tf_op jit(solution)/shard_map/all_gather | solution.py:94
  84.2 77.4 %copy-start.16 = (bf16[2880,128]{1,0:T(8,128)(2,1)}, bf16[2880,128]{1,0:T(8,128)(2,1)S(1)}, u32[]{:S(2)}) copy-start(bf16[2880,128]{1,0:T(8,128)(2,1)S(1)} %reshape.296) | copy-start | bytes 2211844
  85.7 6.1 collective-permute-start
  91.8 72.1 %copy-start.30 = (bf16[256,128]{0,1:T(8,128)(2,1)}, bf16[256,128]{0,1:T(8,128)(2,1)S(1)}, u32[]{:S(2)}) copy-start(bf16[256,128]{0,1:T(8,128)(2,1)S(1)} %copy.68) | copy-start | bytes 196612
  163.6 155.1 %copy-start.28 = (bf16[128,256]{0,1:T(8,128)(2,1)}, bf16[128,256]{0,1:T(8,128)(2,1)S(1)}, u32[]{:S(2)}) copy-start(bf16[128,256]{0,1:T(8,128)(2,1)S(1)} %copy.69) | copy-start | bytes 196612
  163.9 154.8 %copy-start.20 = (f32[1,4,128,256]{2,3,1,0:T(8,128)}, f32[1,4,128,256]{2,3,1,0:T(8,128)S(1)}, u32[]{:S(2)}) copy-start(f32[1,4,128,256]{2,3,1,0:T(8,128)S(1)} %get-tuple-element.46) | copy-start | bytes 1572868
  318.7 2.9 copy-start.33
  318.7 5.0 copy-start.7
  321.6 2.2 copy-start.38
  340.6 117.4 %all-to-all-start.2 = ((bf16[32,20,2880]{2,1,0:T(8,128)(2,1)}), bf16[32,20,2880]{2,1,0:T(8,128)(2,1)}, u32[]{:S(2)}, u32[]{:S(2)}) async-start(bf16[32,20,2880]{2,1,0:T(8,128)(2,1)} %reshape.285), calls=%async_computation.2 | async-start | bytes 9043968 | tf_op jit(solution)/shard_map/all_to_all | solution.py:101
  458.1 69.5 %all-to-all-start = ((bf16[32,20,2880]{2,1,0:T(8,128)(2,1)}), bf16[32,20,2880]{2,1,0:T(8,128)(2,1)}, u32[]{:S(2)}, u32[]{:S(2)}) async-start(bf16[32,20,2880]{2,1,0:T(8,128)(2,1)} %reshape.281), calls=%async_computation | async-start | bytes 9043968 | tf_op jit(solution)/shard_map/all_to_all | solution.py:101
  465.5 292.2 %all-gather.18.cloned.1.call-start = ((), (), s32[]{:S(2)}) async-start(), calls=%async_computation.6 | async-start | bytes 6635520 | tf_op jit(solution)/shard_map/all_gather | solution.py:94
  534.1 3.8 copy-start.13
  534.1 4.1 copy-start.18
  538.2 2.1 copy-start.12
  541.6 1.4 copy-start.26
  541.6 1.4 copy-start.24
  541.6 90.6 %copy-start.22 = (bf16[640,256]{1,0:T(8,128)(2,1)}, bf16[640,256]{1,0:T(8,128)(2,1)S(1)}, u32[]{:S(2)}) copy-start(bf16[640,256]{1,0:T(8,128)(2,1)S(1)} %get-tuple-element.38) | copy-start | bytes 983044
  541.6 1.7 copy-start.19
  632.1 197.2 %all-gather.16.cloned.1.call-start = ((), (), s32[]{:S(2)}) async-start(), calls=%async_computation.5 | async-start | bytes 6635520 | tf_op jit(solution)/shard_map/all_gather | solution.py:94
  757.6 258.5 %all-gather.20.cloned.1.call-start = ((), (), s32[]{:S(2)}) async-start(), calls=%async_computation.7 | async-start | bytes 6635520 | tf_op jit(solution)/shard_map/all_gather | solution.py:94
  761.9 13.3 %copy-start.11 = (bf16[2880,256]{1,0:T(8,128)(2,1)S(1)}, bf16[2880,256]{1,0:T(8,128)(2,1)}, u32[]{:S(2)}) copy-start(bf16[2880,256]{1,0:T(8,128)(2,1)} %reshape.300) | copy-start | bytes 4423684
  774.2 2.8 copy-start.4
  774.2 1.4 copy-start.8
  775.6 2.3 copy-start.21
  779.1 5.1 copy-start.31
  779.1 5.2 copy-start.3
  780.5 5.8 collective-permute-start.1
  784.4 2.0 copy-start.17
  786.4 2.5 copy-start.23
  788.9 5.0 copy-start.14
  788.9 5.0 copy-start.25
  793.9 2.5 copy-start.27
  829.3 6.8 copy-start.5
  829.3 6.8 copy-start.9
  829.3 6.8 copy-start.35
  958.3 49.1 %collective-permute-start.4 = (bf16[96,128]{1,0:T(8,128)(2,1)S(1)}, bf16[96,128]{1,0:T(8,128)(2,1)S(1)}, u32[]{:S(2)}, u32[]{:S(2)}) collective-permute-start(bf16[96,128]{1,0:T(8,128)(2,1)S(1)} %get-tuple-element.32), channel_id=1, source_target_pairs={{0,8},{8,16},{16,24},{24,32},{32,40},{40,48},{48,56},{56,64},{64,7... | collective-permute-start | bytes 73736
  961.0 44.5 %collective-permute-start.5 = (bf16[90,128]{1,0:T(8,128)(2,1)S(1)}, bf16[90,128]{1,0:T(8,128)(2,1)S(1)}, u32[]{:S(2)}, u32[]{:S(2)}) collective-permute-start(bf16[90,128]{1,0:T(8,128)(2,1)S(1)} %slice.57), channel_id=1, source_target_pairs={{0,16},{8,24},{16,32},{24,40},{32,48},{40,56},{48,64},{56,72},{64,... | collective-permute-start | bytes 69128
  985.9 27.9 %collective-permute-start.2 = (bf16[96,256]{1,0:T(8,128)(2,1)S(1)}, bf16[96,256]{1,0:T(8,128)(2,1)S(1)}, u32[]{:S(2)}, u32[]{:S(2)}) collective-permute-start(bf16[96,256]{1,0:T(8,128)(2,1)S(1)} %get-tuple-element.31), channel_id=1, source_target_pairs={{0,8},{8,16},{16,24},{24,32},{32,40},{40,48},{48,56},{56,64},{64,7... | collective-permute-start | bytes 147464
  988.7 25.6 %collective-permute-start.6 = (bf16[256,96]{0,1:T(8,128)(2,1)S(1)}, bf16[256,96]{0,1:T(8,128)(2,1)S(1)}, u32[]{:S(2)}, u32[]{:S(2)}) collective-permute-start(bf16[256,96]{0,1:T(8,128)(2,1)S(1)} %get-tuple-element.33), channel_id=1, source_target_pairs={{0,8},{8,16},{16,24},{24,32},{32,40},{40,48},{48,56},{56,64},{64,7... | collective-permute-start | bytes 147464
  993.7 20.7 %collective-permute-start.7 = (bf16[256,90]{0,1:T(8,128)(2,1)S(1)}, bf16[256,90]{0,1:T(8,128)(2,1)S(1)}, u32[]{:S(2)}, u32[]{:S(2)}) collective-permute-start(bf16[256,90]{0,1:T(8,128)(2,1)S(1)} %slice.58), channel_id=1, source_target_pairs={{0,16},{8,24},{16,32},{24,40},{32,48},{40,56},{48,64},{56,72},{64,... | collective-permute-start | bytes 138248
  1005.5 8.4 collective-permute-start.3
  1020.3 12.8 %copy-start.15 = (bf16[128,2880]{0,1:T(8,128)(2,1)S(1)}, bf16[128,2880]{0,1:T(8,128)(2,1)}, u32[]{:S(2)}) copy-start(bf16[128,2880]{0,1:T(8,128)(2,1)} %bitcast_reduce_fusion.2) | copy-start | bytes 2211844
  1033.9 2.0 copy-start.1
  (7 other events, 7.8 us)
Sparse Core Ops, SparseCore 0:
  9.8 148.4 all-gather.21
  160.1 155.1 all-gather.23
  321.7 103.9 all-gather.13
  632.2 88.3 all-gather.17
  757.7 71.5 all-gather.15
  831.6 69.9 all-gather.19
